TPU v7x, 512 devices: a whole 4x4x16 slice. The times are simulated.
512 devices in a mesh: dp: 32 (over y, x, core), tensor: 16 (over z).
Axes of the slice: x: 4, y: 4, z: 16, core: 2. Of those that a mesh axis runs over, the one named last changes fastest.
Arguments:
- rows_in: bfloat16 [16384, 8192], P('dp', 'tensor'), may hold values from -6 to 6
- adapter_ids: int32 [16384], P('dp'), may hold values from 0 to 511, as said below
- row_counts: int32 [32], P('dp'), may hold values from 256 to 512, as said below
- adapter_slot: int32 [512], replicated, may hold values from 0 to 511, each once
- adapter_a: bfloat16 [512, 16, 16], P(('dp', 'tensor')), may hold values from -1.5 to 1.5
- adapter_b: bfloat16 [512, 512, 1792], P(('dp', 'tensor')), may hold values from -0.25 to 0.25
Outputs:
- delta: bfloat16 [16384, 28672], P('dp', 'tensor')
Inputs may be any that keep to these rules, and one draw needn't show every extreme that they name: `adapter_ids`: within the 512 rows of one dp group (live or not), every adapter that is named is named by exactly 2 rows; some adapter is named by 2 live rows in every group. The live rows of a group are its first row_counts rows; some group has all 512 rows live. `adapter_slot`: each storage index appears once; storage index s is held by the device whose flattened dp, tensor index is s.
All inputs are finite; a program needn't handle non-finite values.
Results may differ from a plain program's by a relative error of at most 0.0049.
Values may be sent and summed in bfloat16 or wider, within the bound.
A program may use at most 128 MiB of HBM per device.

v0:
```python
import jax
import jax.numpy as jnp
from jax import lax
from jax.sharding import PartitionSpec as P

FA = 16
BIN = 512
BOUT = 1792


def on_device(rows_in, adapter_ids, row_counts, adapter_slot, adapter_a, adapter_b):
    group_count = lax.axis_size("dp")
    tensor_count = lax.axis_size("tensor")
    owner_count = group_count * tensor_count
    group_rows, feature_cols = rows_in.shape
    cap = max(2, group_rows // owner_count)
    catalog = jnp.arange(adapter_slot.shape[0], dtype=jnp.int32)
    id_match = adapter_ids[:, None] == catalog[None, :]
    owner_dev = jnp.sum(jnp.where(id_match, adapter_slot[None, :], 0), axis=1)
    position = jnp.arange(group_rows, dtype=jnp.int32)
    row_live = position < row_counts[0]
    earlier_same = (
        (owner_dev[:, None] == owner_dev[None, :])
        & (position[None, :] < position[:, None])
        & row_live[None, :]
    )
    slot_rank = jnp.sum(earlier_same.astype(jnp.int32), axis=1)
    slot_index = owner_dev * cap + slot_rank
    target = jnp.where(row_live, slot_index, owner_count * cap)
    buffer = (
        jnp.zeros((owner_count * cap, feature_cols), jnp.bfloat16)
        .at[target]
        .set(rows_in, mode="drop")
    )
    buffer = buffer.reshape(group_count, tensor_count, cap, feature_cols)
    arrived = lax.all_to_all(
        lax.all_to_all(buffer, "dp", split_axis=0, concat_axis=0, tiled=True),
        "tensor",
        split_axis=1,
        concat_axis=3,
        tiled=True,
    )
    whole_rows = arrived.reshape(group_count * cap, FA, BIN)
    mixed = jnp.einsum(
        "rij,ik->rkj", whole_rows, adapter_a[0], preferred_element_type=jnp.float32
    ).astype(jnp.bfloat16)
    result = jnp.dot(
        mixed.reshape(group_count * cap * FA, BIN), adapter_b[0], preferred_element_type=jnp.float32
    )
    result = result.astype(jnp.bfloat16).reshape(group_count, 1, cap, FA * BOUT)
    split_back = lax.all_to_all(result, "tensor", split_axis=3, concat_axis=1, tiled=True)
    returned = lax.all_to_all(split_back, "dp", split_axis=0, concat_axis=0, tiled=True)
    returned = returned.reshape(owner_count * cap, returned.shape[3])
    picked = jnp.take(returned, jnp.where(row_live, slot_index, 0), axis=0)
    return jnp.where(row_live[:, None], picked, jnp.zeros_like(picked))


def solution(mesh):
    return jax.shard_map(
        on_device,
        mesh=mesh,
        in_specs=(
            P("dp", "tensor"),
            P("dp"),
            P("dp"),
            P(),
            P(("dp", "tensor"), None, None),
            P(("dp", "tensor"), None, None),
        ),
        out_specs=P("dp", "tensor"),
        check_vma=False,
    )
```

profile of v0, /device:TPU:32, one launch (start us, length us, event | category | flops | bytes accessed | tf_op | source)
XLA Modules:
  0.0 458.7 jit_solution(2098749917473446583)
XLA Ops:
  0.0 0.0 copy-start
  0.8 0.9 select_reduce_fusion
  1.7 0.3 convert_reduce_fusion
  2.1 3.2 scatter_custom_fusion
  5.3 1.2 reshape.90
  6.5 24.7 %all_to_all.43 = bf16[32,16,2,512]{3,2,1,0:T(2,128)(2,1)S(1)} all-to-all(bf16[32,16,2,512]{3,2,1,0:T(2,128)(2,1)} %reshape.90), channel_id=1, replica_groups=mesh['dp'=32,'tensor'=16] {'dp'}, dimensions={0} | all-to-all | bytes 2097152 | tf_op jit(solution)/shard_map/all_to_all | solution.py:37
  31.2 1.0 copy.22
  32.1 0.0 copy-start.2
  32.1 66.4 %all_to_all.44 = bf16[32,16,2,512]{3,2,0,1:T(2,128)(2,1)S(1)} all-to-all(bf16[32,16,2,512]{3,2,0,1:T(2,128)(2,1)S(1)} %copy.22), channel_id=1, replica_groups=mesh['dp'=32,'tensor'=16] {'tensor'}, dimensions={1} | all-to-all | bytes 2097152 | tf_op jit(solution)/shard_map/all_to_all | solution.py:36
  98.5 0.9 copy.23
  99.4 0.0 copy-done.2
  99.4 0.5 convolution_convert_fusion.1
  99.8 0.0 copy-done
  99.9 3.9 convolution_convert_fusion
  103.7 8.4 %reshape.93 = bf16[32,1,2,28672]{3,2,0,1:T(2,128)(2,1)} reshape(bf16[1024,1792]{1,0:T(8,128)(2,1)} %convolution_convert_fusion) | data formatting | bytes 7340032 | tf_op jit(solution)/shard_map/reshape | solution.py:50
  112.1 34.8 %copy.25 = bf16[32,1,2,28672]{0,2,1,3:T(2,128)(2,1)} copy(bf16[32,1,2,28672]{3,2,0,1:T(2,128)(2,1)} %reshape.93) | data formatting | bytes 7340032 | tf_op jit(solution)/shard_map/reshape | solution.py:50
  147.0 19.3 %reshape.114 = bf16[16,2,57344]{2,1,0:T(2,128)(2,1)} reshape(bf16[28672,1,2,32]{3,2,1,0:T(2,128)(2,1)} %bitcast.30) | data formatting | bytes 7340032
  166.3 170.2 %all_to_all.45 = bf16[16,2,57344]{2,1,0:T(2,128)(2,1)} all-to-all(bf16[16,2,57344]{2,1,0:T(2,128)(2,1)} %reshape.114), channel_id=1, replica_groups=mesh['dp'=32,'tensor'=16] {'tensor'}, dimensions={0} | all-to-all | bytes 7340032 | tf_op jit(solution)/shard_map/all_to_all | solution.py:51
  336.5 15.6 %reshape.115 = bf16[28672,1,2,32]{3,2,1,0:T(2,128)(2,1)} reshape(bf16[16,2,57344]{2,1,0:T(2,128)(2,1)} %all_to_all.45) | data formatting | bytes 7340032
  352.1 35.1 %copy.26 = bf16[32,1,2,16,1792]{4,2,3,0,1:T(2,128)(2,1)} copy(bf16[32,1,2,16,1792]{0,2,4,3,1:T(2,128)(2,1)} %bitcast.31) | data formatting | bytes 7340032 | tf_op jit(solution)/shard_map/all_to_all | solution.py:51
  387.1 5.0 %all-to-all-start.3 = ((bf16[32,16,2,1792]{3,2,1,0:T(2,128)(2,1)}), bf16[32,16,2,1792]{3,2,1,0:T(2,128)(2,1)}, u32[]{:S(2)}, u32[]{:S(2)}) async-start(bf16[32,16,2,1792]{3,2,1,0:T(2,128)(2,1)} %bitcast.32), calls=%async_computation.3 | async-start | bytes 7340032 | tf_op jit(solution)/shard_map/all_to_all | solution.py:52
  392.2 47.5 %all-to-all-done.3 = bf16[32,16,2,1792]{3,2,1,0:T(2,128)(2,1)} async-done(((bf16[32,16,2,1792]{3,2,1,0:T(2,128)(2,1)}), bf16[32,16,2,1792]{3,2,1,0:T(2,128)(2,1)}, u32[]{:S(2)}, u32[]{:S(2)}) %all-to-all-start.3) | async-done | bytes 3670048 | tf_op jit(solution)/shard_map/all_to_all | solution.py:52
  439.7 8.6 %reshape.94 = bf16[1024,1792]{1,0:T(8,128)(2,1)} reshape(bf16[32,16,2,1792]{3,2,1,0:T(2,128)(2,1)} %all-to-all-done.3) | data formatting | bytes 7340032 | tf_op jit(solution)/shard_map/reshape | solution.py:53
  448.3 7.3 %gather_fusion = bf16[512,1792]{1,0:T(8,128)(2,1)} fusion(bf16[1024,1792]{1,0:T(8,128)(2,1)} %reshape.94, s32[1024]{0:T(1024)S(1)} %pad_clamp_fusion), kind=kCustom, calls=%fused_computation | custom fusion | bytes 3672064 | tf_op jit(solution)/shard_map/jit(_take)/gather | solution.py:54
  455.5 0.0 copy-start.1
  455.5 3.2 select_select_fusion
  458.7 0.0 copy-done.1
  (4 shorter events, 0.0 us)
Async XLA Ops:
  0.0 99.8 %copy-start = (bf16[1,512,1792]{2,1,0:T(8,128)(2,1)S(1)}, bf16[1,512,1792]{2,1,0:T(8,128)(2,1)}, u32[]{:S(2)}) copy-start(bf16[1,512,1792]{2,1,0:T(8,128)(2,1)} %param.11) | copy-start | bytes 5505028
  32.1 67.2 %copy-start.2 = (bf16[1,16,16]{2,1,0:T(8,128)(2,1)S(1)}, bf16[1,16,16]{2,1,0:T(8,128)(2,1)}, u32[]{:S(2)}) copy-start(bf16[1,16,16]{2,1,0:T(8,128)(2,1)} %param.10) | copy-start | bytes 1540
  387.1 52.5 %all-to-all-start.3 = ((bf16[32,16,2,1792]{3,2,1,0:T(2,128)(2,1)}), bf16[32,16,2,1792]{3,2,1,0:T(2,128)(2,1)}, u32[]{:S(2)}, u32[]{:S(2)}) async-start(bf16[32,16,2,1792]{3,2,1,0:T(2,128)(2,1)} %bitcast.32), calls=%async_computation.3 | async-start | bytes 7340032 | tf_op jit(solution)/shard_map/all_to_all | solution.py:52
  455.5 3.2 copy-start.1
where the time goes:
time: 464 us; the launch traced here: 459 us
  blocking collectives  261 us (56%)
  local copies, waits for them, and re-layouts  135 us (29%)
  waiting for transfers between devices  47.5 us (10%)
  starting transfers between devices  5.01 us (1%)
    all_to_all x1, blocking collectives, on_device(): lax.all_to_all(result, 'tensor', split_axis=3, concat_axis=1, tiled=True)  170 us
    all_to_all x1, blocking collectives, on_device(): lax.all_to_all(lax.all_to_all(buffer, 'dp', split_axis=0, concat_axis=0,...  66.4 us
    all_to_all x1, waiting for transfers between devices, on_device(): lax.all_to_all(split_back, 'dp', split_axis=0, concat_axis=0, tiled=True)  47.5 us
    reshape x2, local copies, waits for them, and re-layouts, on_device(): result = result.astype(jnp.bfloat16).reshape(group_count, 1, cap, FA * BOUT)  43.3 us
    all_to_all x1, local copies, waits for them, and re-layouts, on_device(): lax.all_to_all(result, 'tensor', split_axis=3, concat_axis=1, tiled=True)  35.1 us
    unnamed x8, local copies, waits for them, and re-layouts  34.9 us
    all_to_all x1, blocking collectives, on_device(): lax.all_to_all(buffer, 'dp', split_axis=0, concat_axis=0, tiled=True)  24.7 us
  transfers between devices with their start and end apart: 1, of which 1 were waited for; matrix products, arithmetic and copies ran while one was open for 0% of the time, Pallas kernels for 0%

commit v1 on v0

--- a/solution.py
+++ b/solution.py
@@ -6,6 +6,23 @@
 FA = 16
 BIN = 512
 BOUT = 1792
+
+
+def spread_pages(my_data, k_dim, frame):
+    block_now = my_data.shape
+    return jnp.moveaxis(
+        my_data.reshape(
+            *block_now[:k_dim], frame, block_now[k_dim] // frame, *block_now[k_dim + 1 :]
+        ),
+        k_dim,
+        0,
+    )
+
+
+def choose_figure(vector, at_axis):
+    earlier = list(vector.shape[1:])
+    earlier[at_axis] *= vector.shape[0]
+    return jnp.moveaxis(vector, 0, at_axis).reshape(earlier)
 
 
 def on_device(rows_in, adapter_ids, row_counts, adapter_slot, adapter_a, adapter_b):
@@ -48,7 +65,15 @@
         mixed.reshape(group_count * cap * FA, BIN), adapter_b[0], preferred_element_type=jnp.float32
     )
     result = result.astype(jnp.bfloat16).reshape(group_count, 1, cap, FA * BOUT)
-    split_back = lax.all_to_all(result, "tensor", split_axis=3, concat_axis=1, tiled=True)
+    f_now = lax.axis_size("tensor")
+    value_now, val2 = (f_now, lax.axis_index("tensor"))
+    mixed_arr = spread_pages(result, 3, value_now)
+    entries = [mixed_arr[val2]]
+    for q in range(1, value_now):
+        shaped = mixed_arr[val2 ^ q]
+        entries.append(lax.ppermute(shaped, "tensor", [(j, j ^ q) for j in range(value_now)]))
+    mixed_arr = jnp.stack(entries)[val2 ^ jnp.arange(value_now)]
+    split_back = choose_figure(mixed_arr, 1)
     returned = lax.all_to_all(split_back, "dp", split_axis=0, concat_axis=0, tiled=True)
     returned = returned.reshape(owner_count * cap, returned.shape[3])
     picked = jnp.take(returned, jnp.where(row_live, slot_index, 0), axis=0)

time: 464 us -> 449 us (0.968)
  the two profiles are of different devices: /device:TPU:32 before, /device:TPU:1 now
where the time goes in v1:
time: 449 us; the launch traced here: 448 us
  starting transfers between devices  190 us (42%)
  waiting for transfers between devices  164 us (37%)
  local copies, waits for them, and re-layouts  58.1 us (13%)
  blocking collectives  27.7 us (6%)
    ppermute x15, starting transfers between devices, on_device(): lax.ppermute(shaped, 'tensor', [(j, j ^ q) for j in range(value_now)])  165 us
    ppermute x15, waiting for transfers between devices, on_device(): lax.ppermute(shaped, 'tensor', [(j, j ^ q) for j in range(value_now)])  74.3 us
    all_to_all x1, waiting for transfers between devices, on_device(): lax.all_to_all(lax.all_to_all(buffer, 'dp', split_axis=0, concat_axis=0,...  45.3 us
    all_to_all x1, waiting for transfers between devices, on_device(): lax.all_to_all(split_back, 'dp', split_axis=0, concat_axis=0, tiled=True)  44.8 us
    all_to_all x1, blocking collectives, on_device(): lax.all_to_all(buffer, 'dp', split_axis=0, concat_axis=0, tiled=True)  27.7 us
    all_to_all x1, starting transfers between devices, on_device(): lax.all_to_all(lax.all_to_all(buffer, 'dp', split_axis=0, concat_axis=0,...  12.9 us
    all_to_all x1, starting transfers between devices, on_device(): lax.all_to_all(split_back, 'dp', split_axis=0, concat_axis=0, tiled=True)  12.4 us
    unnamed x34, local copies, waits for them, and re-layouts  11.2 us
  transfers between devices with their start and end apart: 17, of which 7 were waited for; matrix products, arithmetic and copies ran while one was open for 2% of the time, Pallas kernels for 0%

profile of v1, /device:TPU:1, one launch (start us, length us, event | category | flops | bytes accessed | tf_op | source)
XLA Modules:
  0.0 448.2 jit_solution(6603494177847779742)
XLA Ops:
  2.1 3.2 scatter_custom_fusion
  6.5 27.7 %all_to_all.25 = bf16[32,16,2,512]{3,2,1,0:T(2,128)(2,1)S(1)} all-to-all(bf16[32,16,2,512]{3,2,1,0:T(2,128)(2,1)} %reshape.137), channel_id=1, replica_groups=mesh['dp'=32,'tensor'=16] {'dp'}, dimensions={0} | all-to-all | bytes 2097152 | tf_op jit(solution)/shard_map/all_to_all | solution.py:54
  34.2 2.0 copy.68
  36.2 12.9 %all-to-all-start.1 = ((bf16[32,16,2,512]{3,2,0,1:T(2,128)(2,1)}), bf16[32,16,2,512]{3,2,0,1:T(2,128)(2,1)S(1)}, u32[]{:S(2)}, u32[]{:S(2)}) async-start(bf16[32,16,2,512]{3,2,0,1:T(2,128)(2,1)} %copy.68), calls=%async_computation.1 | async-start | bytes 2097152 | tf_op jit(solution)/shard_map/all_to_all | solution.py:53
  49.3 45.3 %all-to-all-done.1 = bf16[32,16,2,512]{3,2,0,1:T(2,128)(2,1)S(1)} async-done(((bf16[32,16,2,512]{3,2,0,1:T(2,128)(2,1)}), bf16[32,16,2,512]{3,2,0,1:T(2,128)(2,1)S(1)}, u32[]{:S(2)}, u32[]{:S(2)}) %all-to-all-start.1) | async-done | bytes 1048608 | tf_op jit(solution)/shard_map/all_to_all | solution.py:53
  96.0 2.1 convolution_convert_fusion
  98.0 10.8 %constant_dynamic-slice_fusion = (bf16[32,1,2,1,1792]{4,3,2,0,1:T(2,128)(2,1)S(1)}, bf16[32,1,2,1,1792]{4,3,2,0,1:T(2,128)(2,1)S(1)}, bf16[32,1,2,1,1792]{4,3,2,...) fusion(bf16[32,1,2,16,1792]{4,3,2,0,1:T(8,128)(2,1)S(1)} %bitca, ...), kind=kLoop, calls=%fused_computation.55 | loop fusion | bytes 7340096 | tf_op jit(solution)/shard_map/dynamic-slice.15
  109.1 2.9 collective-permute-start
  111.9 5.8 %collective-permute-start.1 = (bf16[32,1,2,1792]{3,0,2,1:T(8,128)(2,1)S(1)}, bf16[32,1,2,1792]{3,0,2,1:T(8,128)(2,1)S(1)}, u32[]{:S(2)}, u32[]{:S(2)}) collective-permute-start(bf16[32,1,2,1792]{3,0,2,1:T(8,128)(2,1)S(1)} %bitcast.132), channel_id=1, source_target_pairs={{0,2},{1,3},{2,0},{3,1},{4,6},{5,7},{6,4},{7,5},{8,10},{9,11},{10,... | collective-permute-start | bytes 688136 | tf_op jit(solution)/shard_map/ppermute | solution.py:74
  119.6 8.9 %collective-permute-start.3 = (bf16[32,1,2,1792]{3,0,2,1:T(8,128)(2,1)S(1)}, bf16[32,1,2,1792]{3,0,2,1:T(8,128)(2,1)S(1)}, u32[]{:S(2)}, u32[]{:S(2)}) collective-permute-start(bf16[32,1,2,1792]{3,0,2,1:T(8,128)(2,1)S(1)} %bitcast.128), channel_id=1, source_target_pairs={{0,4},{1,5},{2,6},{3,7},{4,0},{5,1},{6,2},{7,3},{8,12},{9,13},{10,... | collective-permute-start | bytes 688136 | tf_op jit(solution)/shard_map/ppermute | solution.py:74
  128.5 2.0 collective-permute-start.4
  131.7 9.2 %collective-permute-start.5 = (bf16[32,1,2,1792]{3,0,2,1:T(8,128)(2,1)S(1)}, bf16[32,1,2,1792]{3,0,2,1:T(8,128)(2,1)S(1)}, u32[]{:S(2)}, u32[]{:S(2)}) collective-permute-start(bf16[32,1,2,1792]{3,0,2,1:T(8,128)(2,1)S(1)} %bitcast.133), channel_id=1, source_target_pairs={{0,6},{1,7},{2,4},{3,5},{4,2},{5,3},{6,0},{7,1},{8,14},{9,15},{10,... | collective-permute-start | bytes 688136 | tf_op jit(solution)/shard_map/ppermute | solution.py:74
  141.6 3.6 collective-permute-start.6
  145.9 8.4 %collective-permute-start.7 = (bf16[32,1,2,1792]{3,0,2,1:T(8,128)(2,1)S(1)}, bf16[32,1,2,1792]{3,0,2,1:T(8,128)(2,1)S(1)}, u32[]{:S(2)}, u32[]{:S(2)}) collective-permute-start(bf16[32,1,2,1792]{3,0,2,1:T(8,128)(2,1)S(1)} %bitcast.129), channel_id=1, source_target_pairs={{0,8},{1,9},{2,10},{3,11},{4,12},{5,13},{6,14},{7,15},{8,0},{9,1},... | collective-permute-start | bytes 688136 | tf_op jit(solution)/shard_map/ppermute | solution.py:74
  155.1 21.5 %collective-permute-start.8 = (bf16[32,1,2,1792]{3,0,2,1:T(8,128)(2,1)S(1)}, bf16[32,1,2,1792]{3,0,2,1:T(8,128)(2,1)S(1)}, u32[]{:S(2)}, u32[]{:S(2)}) collective-permute-start(bf16[32,1,2,1792]{3,0,2,1:T(8,128)(2,1)S(1)} %bitcast.127), channel_id=1, source_target_pairs={{0,9},{1,8},{2,11},{3,10},{4,13},{5,12},{6,15},{7,14},{8,1},{9,0},... | collective-permute-start | bytes 688136 | tf_op jit(solution)/shard_map/ppermute | solution.py:74
  177.4 63.7 %collective-permute-start.9 = (bf16[32,1,2,1792]{3,0,2,1:T(8,128)(2,1)S(1)}, bf16[32,1,2,1792]{3,0,2,1:T(8,128)(2,1)S(1)}, u32[]{:S(2)}, u32[]{:S(2)}) collective-permute-start(bf16[32,1,2,1792]{3,0,2,1:T(8,128)(2,1)S(1)} %bitcast.125), channel_id=1, source_target_pairs={{0,10},{1,11},{2,8},{3,9},{4,14},{5,15},{6,12},{7,13},{8,2},{9,3},... | collective-permute-start | bytes 688136 | tf_op jit(solution)/shard_map/ppermute | solution.py:74
  244.4 5.3 %collective-permute-start.11 = (bf16[32,1,2,1792]{3,0,2,1:T(8,128)(2,1)S(1)}, bf16[32,1,2,1792]{3,0,2,1:T(8,128)(2,1)S(1)}, u32[]{:S(2)}, u32[]{:S(2)}) collective-permute-start(bf16[32,1,2,1792]{3,0,2,1:T(8,128)(2,1)S(1)} %bitcast.123), channel_id=1, source_target_pairs={{0,12},{1,13},{2,14},{3,15},{4,8},{5,9},{6,10},{7,11},{8,4},{9,5},... | collective-permute-start | bytes 688136 | tf_op jit(solution)/shard_map/ppermute | solution.py:74
  250.5 3.8 collective-permute-start.12
  255.1 19.2 %collective-permute-start.13 = (bf16[32,1,2,1792]{3,0,2,1:T(8,128)(2,1)S(1)}, bf16[32,1,2,1792]{3,0,2,1:T(8,128)(2,1)S(1)}, u32[]{:S(2)}, u32[]{:S(2)}) collective-permute-start(bf16[32,1,2,1792]{3,0,2,1:T(8,128)(2,1)S(1)} %bitcast.121), channel_id=1, source_target_pairs={{0,14},{1,15},{2,12},{3,13},{4,10},{5,11},{6,8},{7,9},{8,6},{9,7},... | collective-permute-start | bytes 688136 | tf_op jit(solution)/shard_map/ppermute | solution.py:74
  275.0 6.4 %collective-permute-start.14 = (bf16[32,1,2,1792]{3,0,2,1:T(8,128)(2,1)S(1)}, bf16[32,1,2,1792]{3,0,2,1:T(8,128)(2,1)S(1)}, u32[]{:S(2)}, u32[]{:S(2)}) collective-permute-start(bf16[32,1,2,1792]{3,0,2,1:T(8,128)(2,1)S(1)} %bitcast.120), channel_id=1, source_target_pairs={{0,15},{1,14},{2,13},{3,12},{4,11},{5,10},{6,9},{7,8},{8,7},{9,6},... | collective-permute-start | bytes 688136 | tf_op jit(solution)/shard_map/ppermute | solution.py:74
  282.1 52.2 %collective-permute-done.10 = bf16[32,1,2,1792]{3,0,2,1:T(8,128)(2,1)S(1)} collective-permute-done((bf16[32,1,2,1792]{3,0,2,1:T(8,128)(2,1)S(1)}, bf16[32,1,2,1792]{3,0,2,1:T(8,128)(2,1)S(1)}, u32[]{:S(2)}, u32[]{:S(2)}) %collective-permute-start.10) | collective-permute-done | bytes 229408 | tf_op jit(solution)/shard_map/ppermute | solution.py:74
  335.0 4.2 collective-permute-done.11
  339.9 4.2 collective-permute-done.12
  344.8 6.5 %collective-permute-done.13 = bf16[32,1,2,1792]{3,0,2,1:T(8,128)(2,1)S(1)} collective-permute-done((bf16[32,1,2,1792]{3,0,2,1:T(8,128)(2,1)S(1)}, bf16[32,1,2,1792]{3,0,2,1:T(8,128)(2,1)S(1)}, u32[]{:S(2)}, u32[]{:S(2)}) %collective-permute-start.13) | collective-permute-done | bytes 229408 | tf_op jit(solution)/shard_map/ppermute | solution.py:74
  352.1 7.1 %collective-permute-done.14 = bf16[32,1,2,1792]{3,0,2,1:T(8,128)(2,1)S(1)} collective-permute-done((bf16[32,1,2,1792]{3,0,2,1:T(8,128)(2,1)S(1)}, bf16[32,1,2,1792]{3,0,2,1:T(8,128)(2,1)S(1)}, u32[]{:S(2)}, u32[]{:S(2)}) %collective-permute-start.14) | collective-permute-done | bytes 229408 | tf_op jit(solution)/shard_map/ppermute | solution.py:74
  359.9 4.6 %gather_fusion = bf16[16,32,2,1792]{3,1,2,0:T(8,128)(2,1)} fusion(bf16[16,32,2,1792]{3,1,2,0:T(8,128)(2,1)} %bitcast.44, s32[1024]{0:T(1024)S(1)} %pad_clamp_fusion.1), kind=kCustom, calls=%fused_computation | custom fusion | bytes 7340096 | tf_op jit(solution)/shard_map/gather | solution.py:75
  364.5 7.7 %copy.88 = bf16[32,16,2,1792]{3,2,1,0:T(2,128)(2,1)} copy(bf16[32,16,2,1792]{3,0,2,1:T(8,128)(2,1)} %bitcast.116) | data formatting | bytes 7340032 | tf_op jit(solution)/shard_map/reshape | solution.py:25
  372.1 12.4 %all-to-all-start.2 = ((bf16[32,16,2,1792]{3,2,1,0:T(2,128)(2,1)}), bf16[32,16,2,1792]{3,2,1,0:T(2,128)(2,1)}, u32[]{:S(2)}, u32[]{:S(2)}) async-start(bf16[32,16,2,1792]{3,2,1,0:T(2,128)(2,1)} %copy.88), calls=%async_computation.2 | async-start | bytes 7340032 | tf_op jit(solution)/shard_map/all_to_all | solution.py:77
  384.6 44.8 %all-to-all-done.2 = bf16[32,16,2,1792]{3,2,1,0:T(2,128)(2,1)} async-done(((bf16[32,16,2,1792]{3,2,1,0:T(2,128)(2,1)}), bf16[32,16,2,1792]{3,2,1,0:T(2,128)(2,1)}, u32[]{:S(2)}, u32[]{:S(2)}) %all-to-all-start.2) | async-done | bytes 3670048 | tf_op jit(solution)/shard_map/all_to_all | solution.py:77
  429.4 8.6 %reshape.141 = bf16[1024,1792]{1,0:T(8,128)(2,1)} reshape(bf16[32,16,2,1792]{3,2,1,0:T(2,128)(2,1)} %all-to-all-done.2) | data formatting | bytes 7340032 | tf_op jit(solution)/shard_map/reshape | solution.py:78
  438.0 7.3 %gather_fusion.1 = bf16[512,1792]{1,0:T(8,128)(2,1)} fusion(bf16[1024,1792]{1,0:T(8,128)(2,1)} %reshape.141, s32[1024]{0:T(1024)S(1)} %pad_clamp_fusion), kind=kCustom, calls=%fused_computation.1 | custom fusion | bytes 3672064 | tf_op jit(solution)/shard_map/jit(_take)/gather | solution.py:79
  445.2 3.0 select_select_fusion
  (58 shorter events, 19.6 us)
Async XLA Ops:
  0.0 95.9 %copy-start = (bf16[1,512,1792]{2,1,0:T(8,128)(2,1)S(1)}, bf16[1,512,1792]{2,1,0:T(8,128)(2,1)}, u32[]{:S(2)}) copy-start(bf16[1,512,1792]{2,1,0:T(8,128)(2,1)} %param.11) | copy-start | bytes 5505028
  34.2 61.2 %copy-start.1 = (bf16[1,16,16]{2,1,0:T(8,128)(2,1)S(1)}, bf16[1,16,16]{2,1,0:T(8,128)(2,1)}, u32[]{:S(2)}) copy-start(bf16[1,16,16]{2,1,0:T(8,128)(2,1)} %param.10) | copy-start | bytes 1540
  36.2 58.4 %all-to-all-start.1 = ((bf16[32,16,2,512]{3,2,0,1:T(2,128)(2,1)}), bf16[32,16,2,512]{3,2,0,1:T(2,128)(2,1)S(1)}, u32[]{:S(2)}, u32[]{:S(2)}) async-start(bf16[32,16,2,512]{3,2,0,1:T(2,128)(2,1)} %copy.68), calls=%async_computation.1 | async-start | bytes 2097152 | tf_op jit(solution)/shard_map/all_to_all | solution.py:53
  109.1 22.6 %collective-permute-start = (bf16[32,1,2,1792]{3,0,2,1:T(8,128)(2,1)S(1)}, bf16[32,1,2,1792]{3,0,2,1:T(8,128)(2,1)S(1)}, u32[]{:S(2)}, u32[]{:S(2)}) collective-permute-start(bf16[32,1,2,1792]{3,0,2,1:T(8,128)(2,1)S(1)} %bitcast.134), channel_id=1, source_target_pairs={{0,1},{1,0},{2,3},{3,2},{4,5},{5,4},{6,7},{7,6},{8,9},{9,8},{10,11... | collective-permute-start | bytes 688136 | tf_op jit(solution)/shard_map/ppermute | solution.py:74
  111.9 29.7 %collective-permute-start.1 = (bf16[32,1,2,1792]{3,0,2,1:T(8,128)(2,1)S(1)}, bf16[32,1,2,1792]{3,0,2,1:T(8,128)(2,1)S(1)}, u32[]{:S(2)}, u32[]{:S(2)}) collective-permute-start(bf16[32,1,2,1792]{3,0,2,1:T(8,128)(2,1)S(1)} %bitcast.132), channel_id=1, source_target_pairs={{0,2},{1,3},{2,0},{3,1},{4,6},{5,7},{6,4},{7,5},{8,10},{9,11},{10,... | collective-permute-start | bytes 688136 | tf_op jit(solution)/shard_map/ppermute | solution.py:74
  117.7 28.2 %collective-permute-start.2 = (bf16[32,1,2,1792]{3,0,2,1:T(8,128)(2,1)S(1)}, bf16[32,1,2,1792]{3,0,2,1:T(8,128)(2,1)S(1)}, u32[]{:S(2)}, u32[]{:S(2)}) collective-permute-start(bf16[32,1,2,1792]{3,0,2,1:T(8,128)(2,1)S(1)} %bitcast.130), channel_id=1, source_target_pairs={{0,3},{1,2},{2,1},{3,0},{4,7},{5,6},{6,5},{7,4},{8,11},{9,10},{10,... | collective-permute-start | bytes 688136 | tf_op jit(solution)/shard_map/ppermute | solution.py:74
  119.6 35.5 %collective-permute-start.3 = (bf16[32,1,2,1792]{3,0,2,1:T(8,128)(2,1)S(1)}, bf16[32,1,2,1792]{3,0,2,1:T(8,128)(2,1)S(1)}, u32[]{:S(2)}, u32[]{:S(2)}) collective-permute-start(bf16[32,1,2,1792]{3,0,2,1:T(8,128)(2,1)S(1)} %bitcast.128), channel_id=1, source_target_pairs={{0,4},{1,5},{2,6},{3,7},{4,0},{5,1},{6,2},{7,3},{8,12},{9,13},{10,... | collective-permute-start | bytes 688136 | tf_op jit(solution)/shard_map/ppermute | solution.py:74
  128.5 48.8 %collective-permute-start.4 = (bf16[32,1,2,1792]{3,0,2,1:T(8,128)(2,1)S(1)}, bf16[32,1,2,1792]{3,0,2,1:T(8,128)(2,1)S(1)}, u32[]{:S(2)}, u32[]{:S(2)}) collective-permute-start(bf16[32,1,2,1792]{3,0,2,1:T(8,128)(2,1)S(1)} %bitcast.126), channel_id=1, source_target_pairs={{0,5},{1,4},{2,7},{3,6},{4,1},{5,0},{6,3},{7,2},{8,13},{9,12},{10,... | collective-permute-start | bytes 688136 | tf_op jit(solution)/shard_map/ppermute | solution.py:74
  131.7 110.1 %collective-permute-start.5 = (bf16[32,1,2,1792]{3,0,2,1:T(8,128)(2,1)S(1)}, bf16[32,1,2,1792]{3,0,2,1:T(8,128)(2,1)S(1)}, u32[]{:S(2)}, u32[]{:S(2)}) collective-permute-start(bf16[32,1,2,1792]{3,0,2,1:T(8,128)(2,1)S(1)} %bitcast.133), channel_id=1, source_target_pairs={{0,6},{1,7},{2,4},{3,5},{4,2},{5,3},{6,0},{7,1},{8,14},{9,15},{10,... | collective-permute-start | bytes 688136 | tf_op jit(solution)/shard_map/ppermute | solution.py:74
  141.6 102.8 %collective-permute-start.6 = (bf16[32,1,2,1792]{3,0,2,1:T(8,128)(2,1)S(1)}, bf16[32,1,2,1792]{3,0,2,1:T(8,128)(2,1)S(1)}, u32[]{:S(2)}, u32[]{:S(2)}) collective-permute-start(bf16[32,1,2,1792]{3,0,2,1:T(8,128)(2,1)S(1)} %bitcast.131), channel_id=1, source_target_pairs={{0,7},{1,6},{2,5},{3,4},{4,3},{5,2},{6,1},{7,0},{8,15},{9,14},{10,... | collective-permute-start | bytes 688136 | tf_op jit(solution)/shard_map/ppermute | solution.py:74
  145.9 104.6 %collective-permute-start.7 = (bf16[32,1,2,1792]{3,0,2,1:T(8,128)(2,1)S(1)}, bf16[32,1,2,1792]{3,0,2,1:T(8,128)(2,1)S(1)}, u32[]{:S(2)}, u32[]{:S(2)}) collective-permute-start(bf16[32,1,2,1792]{3,0,2,1:T(8,128)(2,1)S(1)} %bitcast.129), channel_id=1, source_target_pairs={{0,8},{1,9},{2,10},{3,11},{4,12},{5,13},{6,14},{7,15},{8,0},{9,1},... | collective-permute-start | bytes 688136 | tf_op jit(solution)/shard_map/ppermute | solution.py:74
  155.1 100.0 %collective-permute-start.8 = (bf16[32,1,2,1792]{3,0,2,1:T(8,128)(2,1)S(1)}, bf16[32,1,2,1792]{3,0,2,1:T(8,128)(2,1)S(1)}, u32[]{:S(2)}, u32[]{:S(2)}) collective-permute-start(bf16[32,1,2,1792]{3,0,2,1:T(8,128)(2,1)S(1)} %bitcast.127), channel_id=1, source_target_pairs={{0,9},{1,8},{2,11},{3,10},{4,13},{5,12},{6,15},{7,14},{8,1},{9,0},... | collective-permute-start | bytes 688136 | tf_op jit(solution)/shard_map/ppermute | solution.py:74
  177.4 97.7 %collective-permute-start.9 = (bf16[32,1,2,1792]{3,0,2,1:T(8,128)(2,1)S(1)}, bf16[32,1,2,1792]{3,0,2,1:T(8,128)(2,1)S(1)}, u32[]{:S(2)}, u32[]{:S(2)}) collective-permute-start(bf16[32,1,2,1792]{3,0,2,1:T(8,128)(2,1)S(1)} %bitcast.125), channel_id=1, source_target_pairs={{0,10},{1,11},{2,8},{3,9},{4,14},{5,15},{6,12},{7,13},{8,2},{9,3},... | collective-permute-start | bytes 688136 | tf_op jit(solution)/shard_map/ppermute | solution.py:74
  241.8 92.5 %collective-permute-start.10 = (bf16[32,1,2,1792]{3,0,2,1:T(8,128)(2,1)S(1)}, bf16[32,1,2,1792]{3,0,2,1:T(8,128)(2,1)S(1)}, u32[]{:S(2)}, u32[]{:S(2)}) collective-permute-start(bf16[32,1,2,1792]{3,0,2,1:T(8,128)(2,1)S(1)} %bitcast.124), channel_id=1, source_target_pairs={{0,11},{1,10},{2,9},{3,8},{4,15},{5,14},{6,13},{7,12},{8,3},{9,2},... | collective-permute-start | bytes 688136 | tf_op jit(solution)/shard_map/ppermute | solution.py:74
  244.4 94.8 %collective-permute-start.11 = (bf16[32,1,2,1792]{3,0,2,1:T(8,128)(2,1)S(1)}, bf16[32,1,2,1792]{3,0,2,1:T(8,128)(2,1)S(1)}, u32[]{:S(2)}, u32[]{:S(2)}) collective-permute-start(bf16[32,1,2,1792]{3,0,2,1:T(8,128)(2,1)S(1)} %bitcast.123), channel_id=1, source_target_pairs={{0,12},{1,13},{2,14},{3,15},{4,8},{5,9},{6,10},{7,11},{8,4},{9,5},... | collective-permute-start | bytes 688136 | tf_op jit(solution)/shard_map/ppermute | solution.py:74
  250.5 93.6 %collective-permute-start.12 = (bf16[32,1,2,1792]{3,0,2,1:T(8,128)(2,1)S(1)}, bf16[32,1,2,1792]{3,0,2,1:T(8,128)(2,1)S(1)}, u32[]{:S(2)}, u32[]{:S(2)}) collective-permute-start(bf16[32,1,2,1792]{3,0,2,1:T(8,128)(2,1)S(1)} %bitcast.122), channel_id=1, source_target_pairs={{0,13},{1,12},{2,15},{3,14},{4,9},{5,8},{6,11},{7,10},{8,5},{9,4},... | collective-permute-start | bytes 688136 | tf_op jit(solution)/shard_map/ppermute | solution.py:74
  255.1 96.3 %collective-permute-start.13 = (bf16[32,1,2,1792]{3,0,2,1:T(8,128)(2,1)S(1)}, bf16[32,1,2,1792]{3,0,2,1:T(8,128)(2,1)S(1)}, u32[]{:S(2)}, u32[]{:S(2)}) collective-permute-start(bf16[32,1,2,1792]{3,0,2,1:T(8,128)(2,1)S(1)} %bitcast.121), channel_id=1, source_target_pairs={{0,14},{1,15},{2,12},{3,13},{4,10},{5,11},{6,8},{7,9},{8,6},{9,7},... | collective-permute-start | bytes 688136 | tf_op jit(solution)/shard_map/ppermute | solution.py:74
  275.0 84.1 %collective-permute-start.14 = (bf16[32,1,2,1792]{3,0,2,1:T(8,128)(2,1)S(1)}, bf16[32,1,2,1792]{3,0,2,1:T(8,128)(2,1)S(1)}, u32[]{:S(2)}, u32[]{:S(2)}) collective-permute-start(bf16[32,1,2,1792]{3,0,2,1:T(8,128)(2,1)S(1)} %bitcast.120), channel_id=1, source_target_pairs={{0,15},{1,14},{2,13},{3,12},{4,11},{5,10},{6,9},{7,8},{8,7},{9,6},... | collective-permute-start | bytes 688136 | tf_op jit(solution)/shard_map/ppermute | solution.py:74
  372.1 57.2 %all-to-all-start.2 = ((bf16[32,16,2,1792]{3,2,1,0:T(2,128)(2,1)}), bf16[32,16,2,1792]{3,2,1,0:T(2,128)(2,1)}, u32[]{:S(2)}, u32[]{:S(2)}) async-start(bf16[32,16,2,1792]{3,2,1,0:T(2,128)(2,1)} %copy.88), calls=%async_computation.2 | async-start | bytes 7340032 | tf_op jit(solution)/shard_map/all_to_all | solution.py:77
